TPU v7x, 32 devices: a whole 2x2x4 slice. The times are simulated.
32 devices in a mesh: side: 2 (over y), group: 4 (over z), cuts: 4 (over x, core).
Axes of the slice: x: 2, y: 2, z: 4, core: 2. Of those that a mesh axis runs over, the one named last changes fastest.
Arguments:
- queries: bfloat16 [64, 4096], P('group', ('side', 'cuts')), may hold values from -8 to 8
- cache_keys: bfloat16 [64, 8, 64, 512], P('group', ('side', 'cuts')), may hold values from -8 to 8
- cache_values: bfloat16 [64, 8, 64, 512], P('group', ('side', 'cuts')), may hold values from -6 to 6
- new_keys: bfloat16 [64, 512], P('group', ('side', 'cuts')), may hold values from -8 to 8
- new_values: bfloat16 [64, 512], P('group', ('side', 'cuts')), may hold values from -6 to 6
- lengths: int32 [64], P('group'), may hold values from 1 to 512, as said below
- head_sinks: float32 [64], P(('side', 'cuts')), may hold values from 0 to 6
- attn_proj: bfloat16 [4096, 2880], P(('side', 'cuts'), 'group'), may hold values from -0.625 to 0.625
- residual_in: bfloat16 [64, 2880], P('group'), may hold values from -8 to 8
- norm_gain: float32 [2880], replicated, may hold values from 0.25 to 1.75
- router: bfloat16 [2880, 32], replicated, may hold values from -0.109375 to 0.109375
- expert_routes: int32 [64, 4], P('group'), may hold values from 0 to 31, all different within a row; in each aligned block of 16 rows (0 to 15, 16 to 31, ...) at most 4 rows name the same one
- expert_gate: bfloat16 [2880, 92160], P(None, ('side', 'group', 'cuts')), may hold values from -0.109375 to 0.109375
- expert_up: bfloat16 [2880, 92160], P(None, ('side', 'group', 'cuts')), may hold values from -0.109375 to 0.109375
- expert_down: bfloat16 [92160, 2880], P(('side', 'group', 'cuts')), may hold values from -0.109375 to 0.109375
- adapter_in: bfloat16 [2880, 32], replicated, may hold values from -0.109375 to 0.109375
- adapter_gate: bfloat16 [32, 92160], P(None, ('side', 'group', 'cuts')), may hold values from -1 to 1
- adapter_up: bfloat16 [32, 92160], P(None, ('side', 'group', 'cuts')), may hold values from -1 to 1
Outputs:
- hidden_out: bfloat16 [64, 2880], P('group', 'cuts')
Inputs may be any that keep to these rules, and one draw needn't show every extreme that they name: `expert_routes`: the 16 requests of one index of group name any one expert at most 4 times, a bound that some block reaches. `lengths`: some request has all 512 positions valid.
All inputs are finite; a program needn't handle non-finite values.
Results may differ from a plain program's by a relative error of at most 0.02.
Values may be sent and summed in bfloat16 or wider, within the bound.
A program may use at most 128 MiB of HBM per device.

v0:
```python
import math

import jax
import jax.numpy as jnp
from jax import lax
from jax.sharding import PartitionSpec as P

FF = 2880
CAP = 4


epsilon = 1e-05


def attention_rows(queries, cache_keys, cache_values, new_keys, new_values, lengths, head_sinks):
    req_count = queries.shape[0]
    kv_count = cache_keys.shape[1]
    head_dim = cache_keys.shape[2]
    cache_len = cache_keys.shape[3]
    head_count = head_sinks.shape[0]
    group_size = head_count // kv_count
    query_rows = queries.reshape(req_count, kv_count, group_size, head_dim)
    fresh_key = new_keys.reshape(req_count, kv_count, head_dim)
    fresh_value = new_values.reshape(req_count, kv_count, head_dim)
    scaling = 1.0 / math.sqrt(head_dim)
    scores = (
        jnp.einsum("rkgd,rkdl->rkgl", query_rows, cache_keys, preferred_element_type=jnp.float32)
        * scaling
    )
    own_score = (
        jnp.einsum("rkgd,rkd->rkg", query_rows, fresh_key, preferred_element_type=jnp.float32)
        * scaling
    )
    validity = (
        lax.broadcasted_iota(jnp.int32, (req_count, 1, 1, cache_len), 3)
        < lengths[:, None, None, None]
    )
    scores = jnp.where(validity, scores, -1e30)
    sink_logit = head_sinks.reshape(1, kv_count, group_size)
    highest = jnp.maximum(jnp.maximum(jnp.max(scores, axis=3), own_score), sink_logit)
    exp_terms = jnp.where(validity, jnp.exp(scores - highest[..., None]), 0.0)
    own_term = jnp.exp(own_score - highest)
    denominator = jnp.sum(exp_terms, axis=3) + own_term + jnp.exp(sink_logit - highest)
    attn_probs = (exp_terms / denominator[..., None]).astype(jnp.bfloat16)
    own_prob = (own_term / denominator).astype(jnp.bfloat16)
    attn_mix = jnp.einsum(
        "rkgl,rkdl->rkgd", attn_probs, cache_values, preferred_element_type=jnp.float32
    )
    attn_mix = (
        attn_mix
        + own_prob.astype(jnp.float32)[..., None] * fresh_value.astype(jnp.float32)[:, :, None, :]
    )
    return attn_mix.astype(jnp.bfloat16).reshape(req_count, head_count * head_dim)


def routing_matrix(expert_table, expert_routes, slot_pos, weights):
    slot_total = CAP
    matched = (expert_routes[None, None, :, :] == expert_table[:, :, None, None]).astype(
        jnp.float32
    )
    slot_hot = (
        slot_pos[:, :, None] == lax.broadcasted_iota(jnp.int32, (1, 1, slot_total), 2)
    ).astype(jnp.float32)
    return jnp.einsum(
        "gjrk,rkc->gjcr",
        matched * weights[None, None, :, :],
        slot_hot,
        precision=lax.Precision.HIGHEST,
    )


def shards(
    queries,
    cache_keys,
    cache_values,
    new_keys,
    new_values,
    lengths,
    head_sinks,
    attn_proj,
    residual_in,
    norm_gain,
    router,
    expert_routes,
    expert_gate,
    expert_up,
    expert_down,
    adapter_in,
    adapter_gate,
    adapter_up,
):
    n_group = lax.axis_size("group")
    n_cuts = lax.axis_size("cuts")
    side_index = lax.axis_index("side")
    cut_index = lax.axis_index("cuts")
    attn_out = attention_rows(
        queries, cache_keys, cache_values, new_keys, new_values, lengths, head_sinks
    )
    req_count = attn_out.shape[0]
    width = residual_in.shape[1]
    quarter = width // n_cuts
    partial_cols = jnp.dot(
        lax.all_gather(attn_out, "group", axis=0, tiled=True),
        attn_proj,
        preferred_element_type=jnp.float32,
    )
    partial_rows = lax.all_to_all(
        partial_cols.astype(jnp.bfloat16), "group", split_axis=0, concat_axis=1, tiled=True
    ).astype(partial_cols.dtype)
    projected = lax.psum(partial_rows.astype(jnp.bfloat16), ("side", "cuts")).astype(jnp.float32)
    middle = residual_in.astype(jnp.float32) + projected
    inverse = lax.rsqrt(jnp.mean(middle * middle, axis=1, keepdims=True) + epsilon)
    normed = (middle * inverse * norm_gain).astype(jnp.bfloat16)
    logits = jnp.dot(normed, router, preferred_element_type=jnp.float32)
    expert_count = router.shape[1]
    chosen = (
        expert_routes[:, :, None] == lax.broadcasted_iota(jnp.int32, (1, 1, expert_count), 2)
    ).astype(jnp.float32)
    picked = jnp.sum(chosen * logits[:, None, :], axis=2)
    raw_gate = jax.nn.sigmoid(picked)
    gate_weights = raw_gate / jnp.sum(raw_gate, axis=1, keepdims=True)
    member = jnp.sum(chosen, axis=1)
    earlier = (
        lax.broadcasted_iota(jnp.int32, (req_count, req_count), 1)
        < lax.broadcasted_iota(jnp.int32, (req_count, req_count), 0)
    ).astype(jnp.float32)
    before = jnp.sum(earlier[:, :, None] * member[None, :, :], axis=1)
    slot_pos = jnp.sum(chosen * before[:, None, :], axis=2).astype(jnp.int32)
    slice_width = expert_gate.shape[1]
    local_count = max(slice_width // FF, 1)
    hidden_local = min(slice_width, FF)
    rank_width = adapter_in.shape[1]
    dest_groups = lax.broadcasted_iota(jnp.int32, (n_group, 1), 0)
    row_base = (side_index * n_group + dest_groups) * n_cuts
    local_table = (row_base + cut_index) * slice_width // FF + lax.broadcasted_iota(
        jnp.int32, (1, local_count), 1
    )
    ones_weight = jnp.ones(gate_weights.shape, jnp.float32)
    gate_cols = expert_gate.reshape(width, local_count, hidden_local)
    up_cols = expert_up.reshape(width, local_count, hidden_local)
    down_rows = expert_down.reshape(local_count, hidden_local, width)
    adapt_gate = adapter_gate.reshape(rank_width, local_count, hidden_local)
    adapt_up = adapter_up.reshape(rank_width, local_count, hidden_local)
    placement = routing_matrix(local_table, expert_routes, slot_pos, ones_weight).astype(
        jnp.bfloat16
    )
    outgoing = jnp.einsum(
        "gjcr,rd->gjcd", placement, normed, preferred_element_type=jnp.float32
    ).astype(jnp.bfloat16)
    row_block = lax.all_to_all(outgoing, "group", split_axis=0, concat_axis=0, tiled=True)
    pre_gate = jnp.einsum(
        "gjcd,djh->gjch", row_block, gate_cols, preferred_element_type=jnp.float32
    )
    pre_up = jnp.einsum("gjcd,djh->gjch", row_block, up_cols, preferred_element_type=jnp.float32)
    low_code = jnp.einsum(
        "gjcd,dr->gjcr", row_block, adapter_in, preferred_element_type=jnp.float32
    ).astype(jnp.bfloat16)
    finish_pre_gate = pre_gate
    finish_pre_up = pre_up
    finish_pre_gate = finish_pre_gate + jnp.einsum(
        "gjcr,rjh->gjch", low_code, adapt_gate, preferred_element_type=jnp.float32
    )
    finish_pre_up = finish_pre_up + jnp.einsum(
        "gjcr,rjh->gjch", low_code, adapt_up, preferred_element_type=jnp.float32
    )
    activated = (
        (finish_pre_up + 1.0) * finish_pre_gate * jax.nn.sigmoid(1.702 * finish_pre_gate)
    ).astype(jnp.bfloat16)
    partial_value = jnp.einsum(
        "gjch,jhd->gjcd", activated, down_rows, preferred_element_type=jnp.float32
    )
    returned = lax.all_to_all(
        partial_value.astype(jnp.bfloat16), "group", split_axis=0, concat_axis=0, tiled=True
    ).astype(partial_value.dtype)
    weighting = routing_matrix(local_table, expert_routes, slot_pos, gate_weights)
    moe_part = jnp.einsum("gjcr,gjcd->rd", weighting, returned, precision=lax.Precision.HIGHEST)
    moe_cols = lax.psum_scatter(
        moe_part.astype(jnp.bfloat16), "cuts", scatter_dimension=1, tiled=True
    )
    moe_total = lax.psum(moe_cols, "side").astype(jnp.float32)
    middle_cols = lax.dynamic_slice_in_dim(middle, cut_index * quarter, quarter, 1)
    return (middle_cols + moe_total).astype(jnp.bfloat16)


def solution(mesh):
    placed = (
        P("group", ("side", "cuts")),
        P("group", ("side", "cuts"), None, None),
        P("group", ("side", "cuts"), None, None),
        P("group", ("side", "cuts")),
        P("group", ("side", "cuts")),
        P("group"),
        P(("side", "cuts")),
        P(("side", "cuts"), "group"),
        P("group", None),
        P(),
        P(),
        P("group", None),
        P(None, ("side", "group", "cuts")),
        P(None, ("side", "group", "cuts")),
        P(("side", "group", "cuts"), None),
        P(),
        P(None, ("side", "group", "cuts")),
        P(None, ("side", "group", "cuts")),
    )
    return jax.shard_map(
        shards, mesh=mesh, in_specs=placed, out_specs=P("group", "cuts"), check_vma=False
    )
```

profile of v0, /device:TPU:0, one launch (start us, length us, event | category | flops | bytes accessed | tf_op | source)
XLA Modules:
  0.0 178.5 jit_solution(12689045732461411870)
XLA Ops:
  6.5 0.8 iota_compare_fusion.4
  7.4 0.7 convert_element_type.103
  8.1 0.8 reshape.235
  8.9 0.8 fusion.55
  9.7 0.3 fusion.64
  10.0 0.7 maximum_maximum_fusion
  10.7 0.2 fusion.23
  10.9 0.7 fusion.58
  11.6 1.7 fusion.19
  13.2 0.1 reshape.238
  13.4 14.9 %all_gather.3 = bf16[64,512]{1,0:T(8,128)(2,1)S(1)} all-gather(bf16[16,512]{1,0:T(8,128)(2,1)S(1)} %reshape.238), channel_id=1, replica_groups=mesh['side'=2,'group'=4,'cuts'=4] {'group'}, dimensions={0}, use_global_device_ids=true | all-gather | bytes 81920 | tf_op jit(solution)/shard_map/all_gather | solution.py:103
  28.3 2.1 %convolution_convert_fusion.1 = bf16[64,720]{1,0:T(8,128)(2,1)} fusion(bf16[64,512]{1,0:T(8,128)(2,1)S(1)} %all_gather.3, bf16[512,720]{0,1:T(8,128)(2,1)} %param.25), kind=kOutput, calls=%fused_computation.20 | convolution fusion | flops 47232000 | bytes 894976 | tf_op jit(solution)/shard_map/dot_general | solution.py:102
  30.3 4.7 %all-to-all-start = ((bf16[4,16,720]{2,1,0:T(8,128)(2,1)}), bf16[4,16,720]{2,1,0:T(8,128)(2,1)S(1)}, u32[]{:S(2)}, u32[]{:S(2)}) async-start(bf16[4,16,720]{2,1,0:T(8,128)(2,1)} %bitcast.5), calls=%async_computation | async-start | bytes 196608 | tf_op jit(solution)/shard_map/all_to_all | solution.py:107
  35.1 0.8 convert_reduce_fusion
  35.9 0.1 multiply_reduce_fusion.1
  36.0 4.9 %all-to-all-done = bf16[4,16,720]{2,1,0:T(8,128)(2,1)S(1)} async-done(((bf16[4,16,720]{2,1,0:T(8,128)(2,1)}), bf16[4,16,720]{2,1,0:T(8,128)(2,1)S(1)}, u32[]{:S(2)}, u32[]{:S(2)}) %all-to-all-start) | async-done | bytes 92192 | tf_op jit(solution)/shard_map/all_to_all | solution.py:107
  40.9 0.1 copy.33
  41.0 0.8 all_to_all.23
  41.7 0.0 all-reduce.2.cloned.1.call-update
  41.8 0.8 copy.35
  42.5 49.5 %all-reduce.2.cloned.1.call-done = bf16[16,2880]{1,0:T(8,128)(2,1)} async-done(((bf16[16,2880]{1,0:T(8,128)(2,1)}), bf16[16,2880]{1,0:T(8,128)(2,1)}) %all-reduce.2.cloned.1.call-update) | async-done | bytes 92176 | tf_op jit(solution)/shard_map/psum | solution.py:110
  92.1 1.1 convert_add_fusion
  93.2 1.3 fusion.63
  94.4 0.9 select_reduce_fusion
  95.3 0.1 copy.34
  95.4 0.2 fusion.20
  95.6 0.1 copy.37
  95.7 1.8 %fusion.14 = bf16[4,1,4,2880]{3,2,1,0:T(4,128)(2,1)} fusion(bf16[4,4,16]{2,1,0:T(4,128)(2,1)S(1)} %copy.37, f32[2880]{0:T(1024)} %param.27, f32[16]{0:T(128)S(1)} %add_rsqrt_fusion, bf16[16,2880]{1,0:T(8,128)(2,1)} %all-reduce.2.cloned.1.call-done, bf16[16,2880]{1,0:T(8,128)(2,1)} %param.26), kind=kOutput, calls=%fused_computation.16 | convolution fusion | flops 1797120 | bytes 288576 | tf_op jit(solution)/shard_map/gjcr,rd->gjcd/dot_general | solution.py:147
  97.6 4.6 %all-to-all-start.1 = ((bf16[4,1,4,2880]{3,2,1,0:T(4,128)(2,1)}), bf16[4,1,4,2880]{3,2,1,0:T(4,128)(2,1)S(1)}, u32[]{:S(2)}, u32[]{:S(2)}) async-start(bf16[4,1,4,2880]{3,2,1,0:T(4,128)(2,1)} %fusion.14), calls=%async_computation.1 | async-start | bytes 188416 | tf_op jit(solution)/shard_map/all_to_all | solution.py:150
  102.2 0.1 copy.36
  102.3 5.8 %all-to-all-done.1 = bf16[4,1,4,2880]{3,2,1,0:T(4,128)(2,1)S(1)} async-done(((bf16[4,1,4,2880]{3,2,1,0:T(4,128)(2,1)}), bf16[4,1,4,2880]{3,2,1,0:T(4,128)(2,1)S(1)}, u32[]{:S(2)}, u32[]{:S(2)}) %all-to-all-start.1) | async-done | bytes 92192 | tf_op jit(solution)/shard_map/all_to_all | solution.py:150
  108.1 1.3 convolution_convert_fusion.3
  109.4 8.8 %fusion.2 = f32[4,4,2880]{2,1,0:T(4,128)S(1)} fusion(bf16[2880,2880]{1,0:T(8,128)(2,1)} %param.30, bf16[4,1,4,2880]{3,2,1,0:T(4,128)(2,1)S(1)} %all-to-all-done.1), kind=kOutput, calls=%fused_computation.2 | convolution fusion | flops 265420800 | bytes 16865280 | tf_op jit(solution)/shard_map/gjcd,djh->gjch/dot_general | solution.py:151
  118.2 0.2 convolution_add_fusion
  118.4 0.4 copy-done.1
  118.8 2.5 %fusion.4 = f32[4,4,2880]{2,1,0:T(4,128)S(1)} fusion(bf16[2880,2880]{1,0:T(8,128)(2,1)S(1)} %copy-done.1, bf16[4,1,4,2880]{3,2,1,0:T(4,128)(2,1)S(1)} %all-to-all-done.1), kind=kOutput, calls=%fused_computation.4 | convolution fusion | flops 265420800 | bytes 16865280 | tf_op jit(solution)/shard_map/gjcd,djh->gjch/dot_general | solution.py:154
  121.3 8.0 %fusion.15 = bf16[4,1,4,2880]{3,2,1,0:T(4,128)(2,1)} fusion(bf16[2880,2880]{1,0:T(8,128)(2,1)} %param.32, f32[4,4,2880]{2,1,0:T(4,128)S(1)} %convolution_add_fusion, f32[4,4,2880]{2,1,0:T(4,128)S(1)} %fusion.4, bf16[4,4,32]{2,1,0:T(4,128)(2,1)S(1)} %convolution_convert_fusion.3, bf16[32,2880]{1,0:T(8,128)(2,1)S(1)} %copy-done.2), kind=kOutput, calls=%fused_computation.17 | convolution fusion | flops 268830720 | bytes 17234944 | tf_op jit(solution)/shard_map/gjch,jhd->gjcd/dot_general | solution.py:169
  129.3 3.3 %all-to-all-start.2 = ((bf16[4,1,4,2880]{3,2,1,0:T(4,128)(2,1)}), bf16[4,1,4,2880]{3,2,1,0:T(4,128)(2,1)S(1)}, u32[]{:S(2)}, u32[]{:S(2)}) async-start(bf16[4,1,4,2880]{3,2,1,0:T(4,128)(2,1)} %fusion.15), calls=%async_computation.2 | async-start | bytes 188416 | tf_op jit(solution)/shard_map/all_to_all | solution.py:172
  132.6 0.0 reduce-scatter.4.cloned.1.call-start
  132.7 0.3 convolution_bitcast_fusion.1
  133.0 5.5 %all-to-all-done.2 = bf16[4,1,4,2880]{3,2,1,0:T(4,128)(2,1)S(1)} async-done(((bf16[4,1,4,2880]{3,2,1,0:T(4,128)(2,1)}), bf16[4,1,4,2880]{3,2,1,0:T(4,128)(2,1)S(1)}, u32[]{:S(2)}, u32[]{:S(2)}) %all-to-all-start.2) | async-done | bytes 92192 | tf_op jit(solution)/shard_map/all_to_all | solution.py:172
  138.4 0.5 fusion.10
  139.0 1.2 copy.44
  140.1 0.0 reduce-scatter.4.cloned.1.call-update
  140.1 21.5 %reduce-scatter.4.cloned.1.call-done = bf16[720,16]{1,0:T(8,128)(2,1)} async-done(((bf16[2880,16]{1,0:T(8,128)(2,1)}), bf16[720,16]{1,0:T(8,128)(2,1)}) %reduce-scatter.4.cloned.1.call-update) | async-done | bytes 23056
  161.7 1.0 copy.45
  162.7 8.3 %psum.15 = bf16[16,720]{1,0:T(8,128)(2,1)S(1)} all-reduce(bf16[16,720]{1,0:T(8,128)(2,1)S(1)} %copy.45), channel_id=1, replica_groups=mesh['side'=2,'group'=4,'cuts'=4] {'side'}, use_global_device_ids=true, to_apply=%region_10.11 | all-reduce | flops 11520 | bytes 46080 | tf_op jit(solution)/shard_map/psum | solution.py:180
  171.0 0.7 add_convert_fusion
  (14 shorter events, 0.1 us)
Async XLA Ops:
  6.5 3.2 %copy-start = (bf16[16,1,64,512]{3,2,1,0:T(8,128)(2,1)S(1)}, bf16[16,1,64,512]{3,2,1,0:T(8,128)(2,1)}, u32[]{:S(2)}) copy-start(bf16[16,1,64,512]{3,2,1,0:T(8,128)(2,1)} %param.19) | copy-start | bytes 3145732
  6.5 111.7 %copy-start.3 = (bf16[32,2880]{1,0:T(8,128)(2,1)S(1)}, bf16[32,2880]{1,0:T(8,128)(2,1)}, u32[]{:S(2)}) copy-start(bf16[32,2880]{1,0:T(8,128)(2,1)} %param.34) | copy-start | bytes 552964
  30.3 10.6 %all-to-all-start = ((bf16[4,16,720]{2,1,0:T(8,128)(2,1)}), bf16[4,16,720]{2,1,0:T(8,128)(2,1)S(1)}, u32[]{:S(2)}, u32[]{:S(2)}) async-start(bf16[4,16,720]{2,1,0:T(8,128)(2,1)} %bitcast.5), calls=%async_computation | async-start | bytes 196608 | tf_op jit(solution)/shard_map/all_to_all | solution.py:107
  35.1 57.0 %all-reduce.2.cloned.1.call-start = ((), (), s32[]{:S(2)}) async-start(), calls=%async_computation.4 | async-start | bytes 188416 | tf_op jit(solution)/shard_map/psum | solution.py:110
  97.6 10.5 %all-to-all-start.1 = ((bf16[4,1,4,2880]{3,2,1,0:T(4,128)(2,1)}), bf16[4,1,4,2880]{3,2,1,0:T(4,128)(2,1)S(1)}, u32[]{:S(2)}, u32[]{:S(2)}) async-start(bf16[4,1,4,2880]{3,2,1,0:T(4,128)(2,1)} %fusion.14), calls=%async_computation.1 | async-start | bytes 188416 | tf_op jit(solution)/shard_map/all_to_all | solution.py:150
  108.1 10.7 %copy-start.1 = (bf16[2880,2880]{1,0:T(8,128)(2,1)S(1)}, bf16[2880,2880]{1,0:T(8,128)(2,1)}, u32[]{:S(2)}) copy-start(bf16[2880,2880]{1,0:T(8,128)(2,1)} %param.31) | copy-start | bytes 49766404
  109.4 12.0 %copy-start.2 = (bf16[32,2880]{1,0:T(8,128)(2,1)S(1)}, bf16[32,2880]{1,0:T(8,128)(2,1)}, u32[]{:S(2)}) copy-start(bf16[32,2880]{1,0:T(8,128)(2,1)} %param.35) | copy-start | bytes 552964
  129.3 9.1 %all-to-all-start.2 = ((bf16[4,1,4,2880]{3,2,1,0:T(4,128)(2,1)}), bf16[4,1,4,2880]{3,2,1,0:T(4,128)(2,1)S(1)}, u32[]{:S(2)}, u32[]{:S(2)}) async-start(bf16[4,1,4,2880]{3,2,1,0:T(4,128)(2,1)} %fusion.15), calls=%async_computation.2 | async-start | bytes 188416 | tf_op jit(solution)/shard_map/all_to_all | solution.py:172
  132.6 29.0 %reduce-scatter.4.cloned.1.call-start = ((), (), s32[]{:S(2)}) async-start(), calls=%async_computation.5 | async-start | bytes 921600
Sparse Core Ops, SparseCore 0:
  41.9 50.1 all-reduce.1
  140.3 21.3 reduce-scatter.3
where the time goes:
time: 179 us; the launch traced here: 178 us
  waiting for transfers between devices  87.3 us (49%)
  matrix products  29.8 us (17%)
  blocking collectives  23.2 us (13%)
  between operations  13.5 us (8%)
  starting transfers between devices  12.7 us (7%)
  other arithmetic  6.63 us (4%)
  local copies, waits for them, and re-layouts  5.38 us (3%)
    psum x1, waiting for transfers between devices, shards(): lax.psum(partial_rows.astype(jnp.bfloat16), ('side', 'cuts'))  49.5 us
    unnamed x3, waiting for transfers between devices  21.6 us
    all_gather x1, blocking collectives, shards(): lax.all_gather(attn_out, 'group', axis=0, tiled=True)  14.9 us
    dot_general x1, matrix products, shards(): jnp.einsum('gjcd,djh->gjch', row_block, gate_cols, preferred_element_type...  8.84 us
    psum x1, blocking collectives, shards(): moe_total = lax.psum(moe_cols, 'side').astype(jnp.float32)  8.28 us
    dot_general x1, matrix products, shards(): jnp.einsum('gjch,jhd->gjcd', activated, down_rows, preferred_element_type...  7.99 us
    all_to_all x1, waiting for transfers between devices, shards(): lax.all_to_all(outgoing, 'group', split_axis=0, concat_axis=0, tiled=True)  5.84 us
    all_to_all x1, waiting for transfers between devices, shards(): lax.all_to_all(partial_value.astype(jnp.bfloat16), 'group', split_axis=0,...  5.47 us
  transfers between devices with their start and end apart: 5, of which 5 were waited for; matrix products, arithmetic and copies ran while one was open for 1% of the time, Pallas kernels for 0%

commit v1 on v0

--- a/solution.py
+++ b/solution.py
@@ -1,8 +1,11 @@
+import functools
 import math
 
 import jax
 import jax.numpy as jnp
 from jax import lax
+from jax.experimental import pallas as pl
+from jax.experimental.pallas import tpu as pltpu
 from jax.sharding import PartitionSpec as P
 
 FF = 2880
@@ -67,6 +70,669 @@
         slot_hot,
         precision=lax.Precision.HIGHEST,
     )
+
+MESH = pl.DeviceIdType.MESH
+F32 = jnp.float32
+BF16 = jnp.bfloat16
+QUARTERS = 4
+
+
+def idiv(value, by):
+    if by & (by - 1) == 0:
+        return lax.shift_right_logical(value, jnp.full_like(value, by.bit_length() - 1))
+    return lax.div(value, jnp.full_like(value, by))
+
+
+def imod(value, by):
+    return value - idiv(value, by) * by
+
+
+def iota(shape, dim):
+    return lax.broadcasted_iota(jnp.int32, shape, dim)
+
+
+def hot(condition):
+    return jnp.where(condition, 1.0, 0.0)
+
+
+def dot(a, b):
+    return jnp.dot(a, b, preferred_element_type=F32)
+
+
+def dot_nt(a, b):
+    return lax.dot_general(a, b, (((1,), (1,)), ((), ())), preferred_element_type=F32)
+
+
+def swap_digits(outer, inner, tail, dtype):
+    size = outer * inner * tail
+    row, col = iota((size, size), 0), iota((size, size), 1)
+    r_in, r_out, r_tail = idiv(row, outer * tail), imod(idiv(row, tail), outer), imod(row, tail)
+    wanted = (r_out * inner + r_in) * tail + r_tail
+    return hot(col == wanted).astype(dtype)
+
+
+def layer_kernel(
+    sizes,
+    len_ref,
+    sink_ref,
+    q_hbm,
+    nk_hbm,
+    nv_hbm,
+    ck_hbm,
+    cv_hbm,
+    proj_hbm,
+    resid_hbm,
+    gain_hbm,
+    router_hbm,
+    routes_hbm,
+    wg_hbm,
+    wu_hbm,
+    wd_hbm,
+    ain_hbm,
+    ag_hbm,
+    au_hbm,
+    out_ref,
+    q_v,
+    nk_v,
+    nv_v,
+    ck_v,
+    cv_v,
+    proj_v,
+    resid_v,
+    gain_v,
+    router_v,
+    routes_v,
+    wg_v,
+    wu_v,
+    wd_v,
+    ain_v,
+    ag_v,
+    au_v,
+    agb,
+    pb,
+    rb,
+    sc,
+    rc,
+    nst,
+    mid,
+    sd,
+    xd,
+    xp,
+    act,
+    yb,
+    yq,
+    se,
+    re,
+    in_sem,
+    w_sem,
+    send_a,
+    recv_a,
+    send_b,
+    recv_b,
+    send_c,
+    recv_c,
+    send_d,
+    recv_d,
+    send_e,
+    recv_e,
+):
+    n_side, n_group, n_cuts, reqs, heads, hd, width, ff, blk, experts, topk, half = sizes
+    plane = n_side * n_cuts
+    total = plane * n_group
+    part = blk // QUARTERS
+    s = lax.axis_index("side")
+    g = lax.axis_index("group")
+    c = lax.axis_index("cuts")
+    d = s * n_cuts + c
+    me = (s * n_group + g) * n_cuts + c
+
+    def at(side, group, cut):
+        return {"side": side, "group": group, "cuts": cut}
+
+    first = [(q_hbm, q_v), (nk_hbm, nk_v), (nv_hbm, nv_v), (ck_hbm, ck_v), (cv_hbm, cv_v)]
+    second = [
+        (proj_hbm, proj_v),
+        (resid_hbm, resid_v),
+        (gain_hbm, gain_v),
+        (routes_hbm, routes_v),
+        (router_hbm, router_v),
+        (ain_hbm, ain_v),
+        (ag_hbm, ag_v),
+        (au_hbm, au_v),
+    ]
+    small = [
+        pltpu.make_async_copy(a, b, in_sem.at[i]) for i, (a, b) in enumerate(first + second)
+    ]
+    for copy in small:
+        copy.start()
+    rows = width // n_group
+    weights = []
+    for m, (a, b) in enumerate(((wg_hbm, wg_v), (wu_hbm, wu_v), (wd_hbm, wd_v))):
+        weights.append(
+            [
+                pltpu.make_async_copy(
+                    a.at[pl.ds(i * rows, rows)], b.at[pl.ds(i * rows, rows)], w_sem.at[m, i]
+                )
+                for i in range(n_group)
+            ]
+        )
+        for copy in weights[-1]:
+            copy.start()
+
+    barrier = pltpu.get_barrier_semaphore()
+
+    def greet(i, carry):
+        other = lax.rem(me + i, total)
+        pl.semaphore_signal(
+            barrier,
+            inc=1,
+            device_id=at(
+                lax.div(other, n_group * n_cuts),
+                lax.rem(lax.div(other, n_cuts), n_group),
+                lax.rem(other, n_cuts),
+            ),
+            device_id_type=MESH,
+        )
+        return carry
+
+    lax.fori_loop(1, total, greet, 0)
+
+    pb[...] = jnp.zeros_like(pb)
+    nst[...] = jnp.zeros_like(nst)
+    sc[...] = jnp.zeros_like(sc)
+    yq[...] = jnp.zeros_like(yq)
+
+    n_rows = reqs * heads
+    for copy in small[:4]:
+        copy.wait()
+    q = q_v[...]
+    q_stack = jnp.concatenate([q[:, h * hd : (h + 1) * hd] for h in range(heads)], axis=0)
+    q_rows = dot(swap_digits(heads, reqs, 1, BF16), q_stack)
+    spread = hot(
+        idiv(iota((n_rows, reqs), 0), heads) == iota((n_rows, reqs), 1)
+    ).astype(BF16)
+    nk_rows = dot(spread, nk_v[...])
+    scaling = 1.0 / math.sqrt(hd)
+    cache = ck_v.shape[2]
+    place = iota((heads, cache), 1)
+    scores = []
+    for r in range(reqs):
+        raw = dot(q_rows[r * heads : (r + 1) * heads].astype(BF16), ck_v[r]) * scaling
+        scores.append(jnp.where(place < len_ref[r], raw, -1e30))
+    scores = jnp.concatenate(scores, axis=0)
+    own = jnp.sum(q_rows * nk_rows, axis=1, keepdims=True) * scaling
+    head_of = iota((heads, 1), 0)
+    sink = jnp.zeros((heads, 1), F32)
+    for h in range(heads):
+        sink = jnp.where(head_of == h, sink_ref[h], sink)
+    sink = jnp.concatenate([sink] * reqs, axis=0)
+    top = jnp.maximum(jnp.maximum(jnp.max(scores, axis=1, keepdims=True), own), sink)
+    terms = jnp.exp(scores - top)
+    own_term = jnp.exp(own - top)
+    denominator = jnp.sum(terms, axis=1, keepdims=True) + own_term + jnp.exp(sink - top)
+    probs = terms / denominator
+    own_prob = (own_term / denominator).astype(BF16).astype(F32)
+    small[4].wait()
+    nv_rows = dot(spread, nv_v[...])
+    mixed = jnp.concatenate(
+        [
+            dot_nt(probs[r * heads : (r + 1) * heads].astype(BF16), cv_v[r])
+            for r in range(reqs)
+        ],
+        axis=0,
+    )
+    mixed = (mixed + own_prob * nv_rows).astype(BF16)
+    mixed = dot(swap_digits(reqs, heads, 1, BF16), mixed)
+    agb[g] = jnp.concatenate(
+        [mixed[h * reqs : (h + 1) * reqs] for h in range(heads)], axis=1
+    ).astype(BF16)
+
+    pl.semaphore_wait(barrier, total - 1)
+
+    sends = []
+    for i in range(1, n_group):
+        to = lax.rem(g + i, n_group)
+        copy = pltpu.make_async_remote_copy(
+            src_ref=agb.at[g],
+            dst_ref=agb.at[g],
+            send_sem=send_a.at[to],
+            recv_sem=recv_a.at[g],
+            device_id=at(s, to, c),
+            device_id_type=MESH,
+        )
+        copy.start()
+        sends.append(copy)
+
+    for copy in small[5:]:
+        copy.wait()
+    routes = routes_v[...]
+    lane_e = iota((reqs, experts), 1)
+    chosen = [hot(routes[:, j : j + 1] == lane_e) for j in range(topk)]
+    member = functools.reduce(jnp.add, chosen)
+    earlier = hot(iota((reqs, reqs), 1) < iota((reqs, reqs), 0)).astype(BF16)
+    before = dot(earlier, member.astype(BF16))
+    n_pack = n_group * n_group * CAP
+    row_e = iota((n_pack, experts), 0)
+    dest = (s * n_group + idiv(row_e, n_group * CAP)) * n_cuts + c
+    picks = hot(iota((n_pack, experts), 1) == dest).astype(BF16)
+    is_member = dot_nt(picks, member.astype(BF16))
+    is_before = dot_nt(picks, before.astype(BF16))
+    slot_of = imod(iota((n_pack, reqs), 0), CAP).astype(F32)
+    placed = is_member * hot(is_before == slot_of)
+    n_stack = n_group * reqs
+    tile_out = hot(
+        imod(iota((reqs, n_stack), 1), reqs) == iota((reqs, n_stack), 0)
+    ).astype(BF16)
+    place_rows = dot(placed.astype(BF16), tile_out)
+    same_blk = imod(idiv(iota((n_pack, n_stack), 0), CAP), n_group) == idiv(
+        iota((n_pack, n_stack), 1), reqs
+    )
+    place_rows = jnp.where(same_blk, place_rows, 0.0).astype(BF16)
+    resid = resid_v[...]
+
+    for i in range(1, n_group):
+        peer = lax.rem(g + i, n_group)
+        pltpu.make_async_remote_copy(
+            src_ref=agb.at[g],
+            dst_ref=agb.at[peer],
+            send_sem=send_a.at[peer],
+            recv_sem=recv_a.at[peer],
+            device_id=at(s, peer, c),
+            device_id_type=MESH,
+        ).wait_recv()
+    gathered = jnp.concatenate([agb[i] for i in range(n_group)], axis=0)
+    pb[:, :blk] = dot(gathered, proj_v[...]).astype(BF16)
+
+    for i in range(1, plane):
+        to = lax.rem(d + i, plane)
+        copy = pltpu.make_async_remote_copy(
+            src_ref=pb.at[
+                pl.ds(pl.multiple_of(lax.div(to, 2) * reqs, reqs), reqs),
+                pl.ds(pl.multiple_of(lax.rem(to, 2) * half, half), half),
+            ],
+            dst_ref=rb.at[d],
+            send_sem=send_b.at[to],
+            recv_sem=recv_b.at[d],
+            device_id=at(lax.div(to, n_cuts), g, lax.rem(to, n_cuts)),
+            device_id_type=MESH,
+        )
+        copy.start()
+        sends.append(copy)
+    row_block, col_half = lax.div(d, 2), lax.rem(d, 2)
+    total_block = pb[
+        pl.ds(pl.multiple_of(row_block * reqs, reqs), reqs),
+        pl.ds(pl.multiple_of(col_half * half, half), half),
+    ].astype(F32)
+    for i in range(1, plane):
+        peer = lax.rem(d + i, plane)
+        pltpu.make_async_remote_copy(
+            src_ref=sc,
+            dst_ref=rb.at[peer],
+            send_sem=send_b.at[peer],
+            recv_sem=recv_b.at[peer],
+            device_id=at(lax.div(peer, n_cuts), g, lax.rem(peer, n_cuts)),
+            device_id_type=MESH,
+        ).wait_recv()
+        total_block = total_block + rb[peer].astype(F32)
+    summed = total_block.astype(BF16)
+    sc[...] = summed
+
+    for i in range(plane):
+        to = lax.rem(d + i, plane)
+
+        def send_sum(to=to):
+            pltpu.make_async_remote_copy(
+                src_ref=sc,
+                dst_ref=rc.at[g, col_half],
+                send_sem=send_c.at[to],
+                recv_sem=recv_c.at[g, col_half],
+                device_id=at(lax.div(to, n_cuts), row_block, lax.rem(to, n_cuts)),
+                device_id_type=MESH,
+            ).start()
+
+        if i == 0:
+            pl.when(row_block != g)(send_sum)
+
+            @pl.when(row_block == g)
+            def _():
+                rc[g, col_half] = summed
+        else:
+            send_sum()
+
+    def sums_from(i, h):
+        pos = 2 * g + h
+        return pltpu.make_async_remote_copy(
+            src_ref=sc,
+            dst_ref=rc.at[i, h],
+            send_sem=send_c.at[0],
+            recv_sem=recv_c.at[i, h],
+            device_id=at(lax.div(pos, n_cuts), i, lax.rem(pos, n_cuts)),
+            device_id_type=MESH,
+        )
+
+    squares = jnp.zeros((reqs, 1), F32)
+    for i in range(n_group):
+        for h in range(2):
+            mine = jnp.logical_and(i == g, 2 * g + h == d)
+
+            @pl.when(jnp.logical_not(mine))
+            def _(i=i, h=h):
+                sums_from(i, h).wait_recv()
+
+    middles = []
+    for i in range(n_group):
+        projected = jnp.concatenate([rc[i, 0], rc[i, 1]], axis=1)[:, :blk].astype(F32)
+        middle = resid[:, i * blk : (i + 1) * blk].astype(F32) + projected
+        mid[i * reqs : (i + 1) * reqs, :] = middle
+        squares = squares + jnp.sum(middle * middle, axis=1, keepdims=True)
+        middles.append(middle)
+    inverse = lax.rsqrt(squares / width + epsilon)
+    gain = gain_v[...]
+    for i in range(n_group):
+        normed = (middles[i] * inverse * gain[:, i * blk : (i + 1) * blk]).astype(BF16)
+        nst[i * reqs : (i + 1) * reqs, :blk] = normed
+
+    packed = dot(place_rows, nst[...]).astype(BF16)
+    pack = n_group * CAP
+    for i in range(n_group):
+        sd[i] = packed[i * pack : (i + 1) * pack]
+    for i in range(1, n_group):
+        to = lax.rem(g + i, n_group)
+        copy = pltpu.make_async_remote_copy(
+            src_ref=sd.at[to],
+            dst_ref=xd.at[g],
+            send_sem=send_d.at[to],
+            recv_sem=recv_d.at[g],
+            device_id=at(s, to, c),
+            device_id_type=MESH,
+        )
+        copy.start()
+        sends.append(copy)
+    xd[g] = sd[g]
+
+    logits = jnp.zeros((reqs, experts), F32)
+    for i in range(n_group):
+        logits = logits + dot(
+            nst[i * reqs : (i + 1) * reqs, :blk], router_v[i * blk : (i + 1) * blk, :]
+        )
+    raw = [jax.nn.sigmoid(jnp.sum(hits * logits, axis=1, keepdims=True)) for hits in chosen]
+    raw_sum = functools.reduce(jnp.add, raw)
+    weight = functools.reduce(jnp.add, [hits * (x / raw_sum) for hits, x in zip(chosen, raw)])
+    weight_hi = weight.astype(BF16)
+    weight_lo = (weight - weight_hi.astype(F32)).astype(BF16)
+    unit = QUARTERS * CAP
+    wide = experts * unit
+    widen = hot(idiv(iota((experts, wide), 1), unit) == iota((experts, wide), 0)).astype(BF16)
+    slot_ok = dot(before.astype(BF16), widen) == imod(iota((reqs, wide), 1), CAP).astype(F32)
+    quarter_of = imod(idiv(iota((reqs, wide), 1), CAP), QUARTERS)
+    combine = []
+    for value in (weight_hi, weight_lo):
+        spread_w = jnp.where(slot_ok, dot(value, widen), 0.0)
+        combine.append(
+            jnp.concatenate(
+                [jnp.where(quarter_of == i, spread_w, 0.0) for i in range(QUARTERS)], axis=0
+            ).astype(BF16)
+        )
+
+    for i in range(1, n_group):
+        peer = lax.rem(g + i, n_group)
+        pltpu.make_async_remote_copy(
+            src_ref=sd.at[peer],
+            dst_ref=xd.at[peer],
+            send_sem=send_d.at[peer],
+            recv_sem=recv_d.at[peer],
+            device_id=at(s, peer, c),
+            device_id_type=MESH,
+        ).wait_recv()
+    arrived = jnp.concatenate([xd[i] for i in range(n_group)], axis=0)
+    swap = swap_digits(n_group, n_group, CAP, BF16)
+    xp[...] = dot(swap, arrived).astype(BF16)
+
+    low = jnp.zeros((pack, ain_v.shape[1]), F32)
+    for i in range(n_group):
+        low = low + dot(xp[i * pack : (i + 1) * pack, :blk], ain_v[i * blk : (i + 1) * blk, :])
+    low = low.astype(BF16)
+
+    for copies in weights[:2]:
+        for copy in copies:
+            copy.wait()
+
+    def hidden_cols(cols):
+        pre_gate = dot(low, ag_v[:, cols])
+        pre_up = dot(low, au_v[:, cols])
+        for i in range(n_group):
+            x = xp[i * pack : (i + 1) * pack, :blk]
+            pre_gate = pre_gate + dot(x, wg_v[i * blk : (i + 1) * blk, cols])
+            pre_up = pre_up + dot(x, wu_v[i * blk : (i + 1) * blk, cols])
+        act[:, cols] = (
+            (pre_up + 1.0) * pre_gate * jax.nn.sigmoid(1.702 * pre_gate)
+        ).astype(BF16)
+
+    step = 512
+    full = ff // step
+
+    def hidden_step(i, carry):
+        hidden_cols(pl.ds(pl.multiple_of(i * step, step), step))
+        return carry
+
+    lax.fori_loop(0, full, hidden_step, 0)
+    if ff % step:
+        hidden_cols(pl.ds(full * step, ff - full * step))
+
+    for copy in weights[2]:
+        copy.wait()
+    chunk = 2 * half
+    for k in range(n_cuts):
+        low_col, high_col = k * chunk, min((k + 1) * chunk, width)
+        yb[:, low_col:high_col] = dot(act[...], wd_v[:, low_col:high_col])
+        values = yb[...]
+        for i in range(QUARTERS):
+            begin = k * blk + i * part
+            yq[i * pack : (i + 1) * pack, :part] = values[:, begin : begin + part].astype(BF16)
+        blocks = dot(swap, yq[...]).astype(BF16)
+        for i in range(n_group):
+            se[k, i] = blocks[i * pack : (i + 1) * pack]
+
+        @pl.when(c == k)
+        def _(k=k):
+            re[me] = se[k, g]
+
+        for dg in range(n_group):
+            for ds in range(n_side):
+                to_s, to_g = lax.rem(s + ds, n_side), lax.rem(g + dg, n_group)
+
+                def send_rows(k=k, to_s=to_s, to_g=to_g):
+                    pltpu.make_async_remote_copy(
+                        src_ref=se.at[k, to_g],
+                        dst_ref=re.at[me],
+                        send_sem=send_e.at[(to_s * n_group + to_g) * n_cuts + k],
+                        recv_sem=recv_e.at[me],
+                        device_id=at(to_s, to_g, k),
+                        device_id_type=MESH,
+                    ).start()
+
+                if dg == 0 and ds == 0:
+                    pl.when(c != k)(send_rows)
+                else:
+                    send_rows()
+
+    def other_of(i):
+        peer = lax.rem(me + i, total)
+        return pltpu.make_async_remote_copy(
+            src_ref=se.at[0, 0],
+            dst_ref=re.at[peer],
+            send_sem=send_e.at[peer],
+            recv_sem=recv_e.at[peer],
+            device_id=at(
+                lax.div(peer, n_group * n_cuts),
+                lax.rem(lax.div(peer, n_cuts), n_group),
+                lax.rem(peer, n_cuts),
+            ),
+            device_id_type=MESH,
+        )
+
+    def receive(i, carry):
+        other_of(i).wait_recv()
+        return carry
+
+    lax.fori_loop(1, total, receive, 0)
+    returned = re[...].reshape(wide, re.shape[2])
+    moe = dot(combine[0], returned) + dot(combine[1], returned)
+    moe = jnp.concatenate(
+        [moe[i * reqs : (i + 1) * reqs, :part] for i in range(QUARTERS)], axis=1
+    )
+    out_ref[...] = (mid[pl.ds(pl.multiple_of(c * reqs, reqs), reqs), :] + moe).astype(BF16)
+
+    for copy in sends:
+        copy.wait_send()
+    for i in range(plane):
+        to = lax.rem(d + i, plane)
+
+        def sum_sent(to=to):
+            pltpu.make_async_remote_copy(
+                src_ref=sc,
+                dst_ref=rc.at[g, col_half],
+                send_sem=send_c.at[to],
+                recv_sem=recv_c.at[g, col_half],
+                device_id=at(lax.div(to, n_cuts), row_block, lax.rem(to, n_cuts)),
+                device_id_type=MESH,
+            ).wait_send()
+
+        if i == 0:
+            pl.when(row_block != g)(sum_sent)
+        else:
+            sum_sent()
+
+    def sent(i, carry):
+        other_of(i).wait_send()
+        return carry
+
+    lax.fori_loop(1, total, sent, 0)
+
+
+def up_to(value, by):
+    return -(-value // by) * by
+
+
+def fused_fits(queries, cache_keys, residual_in, expert_gate, adapter_in, router, routes, sinks):
+    n_side, n_group, n_cuts = (lax.axis_size(name) for name in ("side", "group", "cuts"))
+    reqs, width = residual_in.shape
+    blk = width // n_group
+    heads = sinks.shape[0]
+    return (
+        n_group == n_cuts
+        and n_side == 2
+        and n_group == QUARTERS
+        and cache_keys.shape[1] == 1
+        and expert_gate.shape[1] == FF
+        and router.shape[1] == n_side * n_group * n_cuts
+        and width % (n_group * QUARTERS) == 0
+        and blk % 16 == 0
+        and reqs == 16
+        and CAP * n_group == 16
+        and heads == 8
+        and 3 * width * up_to(FF, 128) * 2 <= 50 * 2**20
+    )
+
+
+def fused(
+    queries,
+    cache_keys,
+    cache_values,
+    new_keys,
+    new_values,
+    lengths,
+    head_sinks,
+    attn_proj,
+    residual_in,
+    norm_gain,
+    router,
+    expert_routes,
+    expert_gate,
+    expert_up,
+    expert_down,
+    adapter_in,
+    adapter_gate,
+    adapter_up,
+):
+    n_side, n_group, n_cuts = (lax.axis_size(name) for name in ("side", "group", "cuts"))
+    reqs, width = residual_in.shape
+    ff = expert_gate.shape[1]
+    heads, hd, cache = head_sinks.shape[0], cache_keys.shape[2], cache_keys.shape[3]
+    blk = width // n_group
+    half = up_to(-(-blk // 2), 128)
+    experts, topk = router.shape[1], expert_routes.shape[1]
+    plane = n_side * n_cuts
+    total = plane * n_group
+    pack = n_group * CAP
+    lanes = up_to(blk // QUARTERS, 128)
+    sizes = (n_side, n_group, n_cuts, reqs, heads, hd, width, ff, blk, experts, topk, half)
+    squeezed = (reqs, hd, cache)
+    gain = norm_gain.reshape(1, width)
+    operands = (
+        queries,
+        new_keys,
+        new_values,
+        cache_keys.reshape(squeezed),
+        cache_values.reshape(squeezed),
+        attn_proj,
+        residual_in,
+        gain,
+        router,
+        expert_routes,
+        expert_gate,
+        expert_up,
+        expert_down,
+        adapter_in,
+        adapter_gate,
+        adapter_up,
+    )
+    dma = pltpu.SemaphoreType.DMA
+    any_space = pl.BlockSpec(memory_space=pl.ANY)
+    smem = pl.BlockSpec(memory_space=pltpu.SMEM)
+    scratch = [pltpu.VMEM(x.shape, x.dtype) for x in operands]
+    scratch += [
+        pltpu.VMEM((n_group, reqs, heads * hd), BF16),
+        pltpu.VMEM((n_group * reqs, 2 * half), BF16),
+        pltpu.VMEM((plane, reqs, half), BF16),
+        pltpu.VMEM((reqs, half), BF16),
+        pltpu.VMEM((n_group, 2, reqs, half), BF16),
+        pltpu.VMEM((n_group * reqs, 2 * half), BF16),
+        pltpu.VMEM((n_group * reqs, blk), F32),
+        pltpu.VMEM((n_group, pack, 2 * half), BF16),
+        pltpu.VMEM((n_group, pack, 2 * half), BF16),
+        pltpu.VMEM((n_group * pack, 2 * half), BF16),
+        pltpu.VMEM((pack, ff), BF16),
+        pltpu.VMEM((pack, width), F32),
+        pltpu.VMEM((QUARTERS * pack, lanes), BF16),
+        pltpu.VMEM((n_cuts, n_group, QUARTERS * CAP, lanes), BF16),
+        pltpu.VMEM((total, QUARTERS * CAP, lanes), BF16),
+        dma((13,)),
+        dma((3, n_group)),
+        dma((n_group,)),
+        dma((n_group,)),
+        dma((plane,)),
+        dma((plane,)),
+        dma((plane,)),
+        dma((n_group, 2)),
+        dma((n_group,)),
+        dma((n_group,)),
+        dma((total,)),
+        dma((total,)),
+    ]
+    return pl.pallas_call(
+        functools.partial(layer_kernel, sizes),
+        out_shape=jax.ShapeDtypeStruct((reqs, blk), BF16),
+        in_specs=[smem, smem] + [any_space] * len(operands),
+        out_specs=pl.BlockSpec(memory_space=pltpu.VMEM),
+        scratch_shapes=scratch,
+        compiler_params=pltpu.CompilerParams(
+            collective_id=0, has_side_effects=True, vmem_limit_bytes=62 * 2**20
+        ),
+        cost_estimate=pl.CostEstimate(
+            flops=6 * pack * width * ff, bytes_accessed=6 * width * ff, transcendentals=0
+        ),
+    )(lengths, head_sinks, *operands)
 
 
 def shards(
@@ -89,6 +755,36 @@
     adapter_gate,
     adapter_up,
 ):
+    if fused_fits(
+        queries,
+        cache_keys,
+        residual_in,
+        expert_gate,
+        adapter_in,
+        router,
+        expert_routes,
+        head_sinks,
+    ):
+        return fused(
+            queries,
+            cache_keys,
+            cache_values,
+            new_keys,
+            new_values,
+            lengths,
+            head_sinks,
+            attn_proj,
+            residual_in,
+            norm_gain,
+            router,
+            expert_routes,
+            expert_gate,
+            expert_up,
+            expert_down,
+            adapter_in,
+            adapter_gate,
+            adapter_up,
+        )
     n_group = lax.axis_size("group")
     n_cuts = lax.axis_size("cuts")
     side_index = lax.axis_index("side")

time: 179 us -> 64.3 us (0.36)
  waiting for transfers between devices: 87.3 us -> 0 us
  Pallas kernels: 0 us -> 52.8 us
  matrix products: 29.8 us -> 0 us
  blocking collectives: 23.2 us -> 0 us
  between operations: 13.5 us -> 0.01 us
  starting transfers between devices: 12.7 us -> 0 us
  other arithmetic: 6.63 us -> 0 us
  local copies, waits for them, and re-layouts: 5.38 us -> 10.4 us
    pallas_call x0 -> x1, Pallas kernels: none -> 52.8 us  [fused(): pl.pallas_call(functools.partial(layer_kernel, sizes), out_shape=jax.Shap...]
    psum x1 -> x0, waiting for transfers between devices: 49.5 us -> none  [shards(): lax.psum(partial_rows.astype(jnp.bfloat16), ('side', 'cuts'))]
    dot_general x14 -> x0, matrix products: 29.8 us -> none  [the longest x1 8.84 us: shards(): jnp.einsum('gjcd,djh->gjch', row_block, gate_cols, preferred_element_type...]
    unnamed x3 -> x0, waiting for transfers between devices: 21.6 us -> none
    all_to_all x3 -> x0, waiting for transfers between devices: 16.2 us -> none  [the longest x1 5.84 us: shards(): lax.all_to_all(outgoing, 'group', split_axis=0, concat_axis=0, tiled=True)]
    all_gather x1 -> x0, blocking collectives: 14.9 us -> none  [shards(): lax.all_gather(attn_out, 'group', axis=0, tiled=True)]
    all_to_all x3 -> x0, starting transfers between devices: 12.6 us -> none  [the longest x1 4.75 us: shards(): lax.all_to_all(partial_cols.astype(jnp.bfloat16), 'group', split_axis=0,...]
    psum x1 -> x0, blocking collectives: 8.28 us -> none  [shards(): moe_total = lax.psum(moe_cols, 'side').astype(jnp.float32)]
  transfers between devices with their start and end apart: 5 -> 0, of which waited for: 5 -> 0; matrix products, arithmetic and copies ran while one was open for 1% -> 0% of each run, Pallas kernels for 0% -> 0%
where the time goes in v1:
time: 64.3 us; the launch traced here: 63.3 us
  Pallas kernels  52.8 us (82%)
  local copies, waits for them, and re-layouts  10.4 us (16%)
    pallas_call x1, Pallas kernels, fused(): pl.pallas_call(functools.partial(layer_kernel, sizes), out_shape=jax.Shap...  52.8 us
    unnamed x5, local copies, waits for them, and re-layouts  9.11 us
    reshape x1, local copies, waits for them, and re-layouts, fused(): gain = norm_gain.reshape(1, width)  1.31 us

profile of v1, /device:TPU:0, one launch (start us, length us, event | category | flops | bytes accessed | tf_op | source)
XLA Modules:
  0.0 63.3 jit_solution(17565458779149982930)
XLA Ops:
  0.0 1.3 %copy.21.routes_hbm = s32[16,4]{1,0:T(8,128)} copy(s32[16,4]{0,1:T(4,128)} %param.29) | data formatting | bytes 512 | tf_op args[11]
  1.3 1.3 %reshape.11.gain_hbm = f32[1,2880]{1,0:T(1,128)} reshape(f32[2880]{0:T(1024)} %param.27) | data formatting | bytes 23040 | tf_op jit(solution)/shard_map/reshape | solution.py:671
  2.7 2.1 %copy.20.router_hbm = bf16[2880,32]{1,0:T(8,128)(2,1)} copy(bf16[2880,32]{0,1:T(8,128)(2,1)} %param.28) | data formatting | bytes 368640 | tf_op args[10]
  4.8 2.1 %copy.22.ain_hbm = bf16[2880,32]{1,0:T(8,128)(2,1)} copy(bf16[2880,32]{0,1:T(8,128)(2,1)} %param.33) | data formatting | bytes 368640 | tf_op args[15]
  6.8 2.3 %copy.19.proj_hbm = bf16[512,720]{1,0:T(8,128)(2,1)} copy(bf16[512,720]{0,1:T(8,128)(2,1)} %param.25) | data formatting | bytes 1474560 | tf_op args[7]
  9.1 52.8 %shard_map.172 = bf16[16,720]{1,0:T(8,128)(2,1)} custom-call(s32[16]{0:T(128)} %len_ref.1, f32[8]{0:T(128)} %sink_ref.1, bf16[16,512]{1,0:T(8,128)(2,1)} %q_hbm.1, bf16[16,64]{1,0:T(8,128)(2,1)} %nk_hbm.1, bf16[16,64]{1,0:T(8,128)(2,1)} %nv_hbm.1, bf16[16,64,512]{2,1,0:T(8,128)(2,1)} %bitcast.2, bf16[16,64,512]{2,1,0:T(8,128)(2,1)} %bitcast.3, ...), custom_call_target="tpu_custom_call" | custom-call | flops 796262400 | bytes 49766400 | tf_op jit(solution)/shard_map/pallas_call | solution.py:723
  61.9 1.3 %copy.24 = bf16[16,720]{1,0:T(8,128)(2,1)} copy(bf16[16,720]{1,0:T(8,128)(2,1)} %shard_map.172) | data formatting | bytes 46080

commit v2 on v1

--- a/solution.py
+++ b/solution.py
@@ -154,6 +154,7 @@
     sc,
     rc,
     nst,
+    rs,
     mid,
     sd,
     xd,
@@ -163,6 +164,8 @@
     yq,
     se,
     re,
+    fs,
+    fr,
     in_sem,
     w_sem,
     send_a,
@@ -175,6 +178,8 @@
     recv_d,
     send_e,
     recv_e,
+    send_f,
+    recv_f,
 ):
     n_side, n_group, n_cuts, reqs, heads, hd, width, ff, blk, experts, topk, half = sizes
     plane = n_side * n_cuts
@@ -185,6 +190,7 @@
     c = lax.axis_index("cuts")
     d = s * n_cuts + c
     me = (s * n_group + g) * n_cuts + c
+    mine_e = g * n_cuts + c
 
     def at(side, group, cut):
         return {"side": side, "group": group, "cuts": cut}
@@ -216,7 +222,9 @@
                 for i in range(n_group)
             ]
         )
-        for copy in weights[-1]:
+
+    def fetch(m):
+        for copy in weights[m]:
             copy.start()
 
     barrier = pltpu.get_barrier_semaphore()
@@ -245,6 +253,7 @@
     n_rows = reqs * heads
     for copy in small[:4]:
         copy.wait()
+    fetch(0)
     q = q_v[...]
     q_stack = jnp.concatenate([q[:, h * hd : (h + 1) * hd] for h in range(heads)], axis=0)
     q_rows = dot(swap_digits(heads, reqs, 1, BF16), q_stack)
@@ -305,8 +314,9 @@
 
     for copy in small[5:]:
         copy.wait()
-    routes = routes_v[...]
-    lane_e = iota((reqs, experts), 1)
+    eye = hot(iota((reqs, reqs), 0) == iota((reqs, reqs), 1)).astype(BF16)
+    routes = dot_nt(eye, routes_v[...].astype(F32).astype(BF16))
+    lane_e = iota((reqs, experts), 1).astype(F32)
     chosen = [hot(routes[:, j : j + 1] == lane_e) for j in range(topk)]
     member = functools.reduce(jnp.add, chosen)
     earlier = hot(iota((reqs, reqs), 1) < iota((reqs, reqs), 0)).astype(BF16)
@@ -329,6 +339,10 @@
     )
     place_rows = jnp.where(same_blk, place_rows, 0.0).astype(BF16)
     resid = resid_v[...]
+    router_t, ain_t = router_v[...], ain_v[...]
+    for i in range(n_group):
+        rs[i, :experts] = router_t[:, i * blk : (i + 1) * blk]
+        rs[i, experts:] = ain_t[:, i * blk : (i + 1) * blk]
 
     for i in range(1, n_group):
         peer = lax.rem(g + i, n_group)
@@ -341,7 +355,7 @@
             device_id_type=MESH,
         ).wait_recv()
     gathered = jnp.concatenate([agb[i] for i in range(n_group)], axis=0)
-    pb[:, :blk] = dot(gathered, proj_v[...]).astype(BF16)
+    pb[:, :blk] = dot_nt(gathered, proj_v[...]).astype(BF16)
 
     for i in range(1, plane):
         to = lax.rem(d + i, plane)
@@ -358,6 +372,7 @@
         )
         copy.start()
         sends.append(copy)
+    fetch(1)
     row_block, col_half = lax.div(d, 2), lax.rem(d, 2)
     total_block = pb[
         pl.ds(pl.multiple_of(row_block * reqs, reqs), reqs),
@@ -399,6 +414,8 @@
         else:
             send_sum()
 
+    fetch(2)
+
     def sums_from(i, h):
         pos = 2 * g + h
         return pltpu.make_async_remote_copy(
@@ -427,7 +444,7 @@
         squares = squares + jnp.sum(middle * middle, axis=1, keepdims=True)
         middles.append(middle)
     inverse = lax.rsqrt(squares / width + epsilon)
-    gain = gain_v[...]
+    gain = gain_v[...].reshape(1, width)
     for i in range(n_group):
         normed = (middles[i] * inverse * gain[:, i * blk : (i + 1) * blk]).astype(BF16)
         nst[i * reqs : (i + 1) * reqs, :blk] = normed
@@ -452,17 +469,18 @@
 
     logits = jnp.zeros((reqs, experts), F32)
     for i in range(n_group):
-        logits = logits + dot(
-            nst[i * reqs : (i + 1) * reqs, :blk], router_v[i * blk : (i + 1) * blk, :]
-        )
+        logits = logits + dot_nt(nst[i * reqs : (i + 1) * reqs, :blk], rs[i, :experts])
     raw = [jax.nn.sigmoid(jnp.sum(hits * logits, axis=1, keepdims=True)) for hits in chosen]
     raw_sum = functools.reduce(jnp.add, raw)
     weight = functools.reduce(jnp.add, [hits * (x / raw_sum) for hits, x in zip(chosen, raw)])
     weight_hi = weight.astype(BF16)
     weight_lo = (weight - weight_hi.astype(F32)).astype(BF16)
     unit = QUARTERS * CAP
-    wide = experts * unit
-    widen = hot(idiv(iota((experts, wide), 1), unit) == iota((experts, wide), 0)).astype(BF16)
+    flank = n_group * n_cuts
+    wide = flank * unit
+    widen = hot(
+        s * flank + idiv(iota((experts, wide), 1), unit) == iota((experts, wide), 0)
+    ).astype(BF16)
     slot_ok = dot(before.astype(BF16), widen) == imod(iota((reqs, wide), 1), CAP).astype(F32)
     quarter_of = imod(idiv(iota((reqs, wide), 1), CAP), QUARTERS)
     combine = []
@@ -488,9 +506,9 @@
     swap = swap_digits(n_group, n_group, CAP, BF16)
     xp[...] = dot(swap, arrived).astype(BF16)
 
-    low = jnp.zeros((pack, ain_v.shape[1]), F32)
+    low = jnp.zeros((pack, ain_v.shape[0]), F32)
     for i in range(n_group):
-        low = low + dot(xp[i * pack : (i + 1) * pack, :blk], ain_v[i * blk : (i + 1) * blk, :])
+        low = low + dot_nt(xp[i * pack : (i + 1) * pack, :blk], rs[i, experts:])
     low = low.astype(BF16)
 
     for copies in weights[:2]:
@@ -535,39 +553,34 @@
 
         @pl.when(c == k)
         def _(k=k):
-            re[me] = se[k, g]
+            re[mine_e] = se[k, g]
 
         for dg in range(n_group):
-            for ds in range(n_side):
-                to_s, to_g = lax.rem(s + ds, n_side), lax.rem(g + dg, n_group)
-
-                def send_rows(k=k, to_s=to_s, to_g=to_g):
-                    pltpu.make_async_remote_copy(
-                        src_ref=se.at[k, to_g],
-                        dst_ref=re.at[me],
-                        send_sem=send_e.at[(to_s * n_group + to_g) * n_cuts + k],
-                        recv_sem=recv_e.at[me],
-                        device_id=at(to_s, to_g, k),
-                        device_id_type=MESH,
-                    ).start()
-
-                if dg == 0 and ds == 0:
-                    pl.when(c != k)(send_rows)
-                else:
-                    send_rows()
+            to_g = lax.rem(g + dg, n_group)
+
+            def send_rows(k=k, to_g=to_g):
+                pltpu.make_async_remote_copy(
+                    src_ref=se.at[k, to_g],
+                    dst_ref=re.at[mine_e],
+                    send_sem=send_e.at[to_g * n_cuts + k],
+                    recv_sem=recv_e.at[mine_e],
+                    device_id=at(s, to_g, k),
+                    device_id_type=MESH,
+                ).start()
+
+            if dg == 0:
+                pl.when(c != k)(send_rows)
+            else:
+                send_rows()
 
     def other_of(i):
-        peer = lax.rem(me + i, total)
+        peer = lax.rem(mine_e + i, flank)
         return pltpu.make_async_remote_copy(
             src_ref=se.at[0, 0],
             dst_ref=re.at[peer],
             send_sem=send_e.at[peer],
             recv_sem=recv_e.at[peer],
-            device_id=at(
-                lax.div(peer, n_group * n_cuts),
-                lax.rem(lax.div(peer, n_cuts), n_group),
-                lax.rem(peer, n_cuts),
-            ),
+            device_id=at(s, lax.div(peer, n_cuts), lax.rem(peer, n_cuts)),
             device_id_type=MESH,
         )
 
@@ -575,9 +588,22 @@
         other_of(i).wait_recv()
         return carry
 
-    lax.fori_loop(1, total, receive, 0)
+    lax.fori_loop(1, flank, receive, 0)
     returned = re[...].reshape(wide, re.shape[2])
-    moe = dot(combine[0], returned) + dot(combine[1], returned)
+    fs[...] = (dot(combine[0], returned) + dot(combine[1], returned)).astype(BF16)
+
+    across = pltpu.make_async_remote_copy(
+        src_ref=fs,
+        dst_ref=fr,
+        send_sem=send_f.at[0],
+        recv_sem=recv_f.at[0],
+        device_id=at(1 - s, g, c),
+        device_id_type=MESH,
+    )
+    across.start()
+    sends.append(across)
+    across.wait_recv()
+    moe = fs[...].astype(F32) + fr[...].astype(F32)
     moe = jnp.concatenate(
         [moe[i * reqs : (i + 1) * reqs, :part] for i in range(QUARTERS)], axis=1
     )
@@ -607,7 +633,7 @@
         other_of(i).wait_send()
         return carry
 
-    lax.fori_loop(1, total, sent, 0)
+    lax.fori_loop(1, flank, sent, 0)
 
 
 def up_to(value, by):
@@ -663,27 +689,25 @@
     half = up_to(-(-blk // 2), 128)
     experts, topk = router.shape[1], expert_routes.shape[1]
     plane = n_side * n_cuts
-    total = plane * n_group
     pack = n_group * CAP
     lanes = up_to(blk // QUARTERS, 128)
     sizes = (n_side, n_group, n_cuts, reqs, heads, hd, width, ff, blk, experts, topk, half)
     squeezed = (reqs, hd, cache)
-    gain = norm_gain.reshape(1, width)
     operands = (
         queries,
         new_keys,
         new_values,
         cache_keys.reshape(squeezed),
         cache_values.reshape(squeezed),
-        attn_proj,
+        attn_proj.T,
         residual_in,
-        gain,
-        router,
-        expert_routes,
+        norm_gain,
+        router.T,
+        expert_routes.T,
         expert_gate,
         expert_up,
         expert_down,
-        adapter_in,
+        adapter_in.T,
         adapter_gate,
         adapter_up,
     )
@@ -698,6 +722,7 @@
         pltpu.VMEM((reqs, half), BF16),
         pltpu.VMEM((n_group, 2, reqs, half), BF16),
         pltpu.VMEM((n_group * reqs, 2 * half), BF16),
+        pltpu.VMEM((n_group, experts + adapter_in.shape[1], blk), BF16),
         pltpu.VMEM((n_group * reqs, blk), F32),
         pltpu.VMEM((n_group, pack, 2 * half), BF16),
         pltpu.VMEM((n_group, pack, 2 * half), BF16),
@@ -706,7 +731,9 @@
         pltpu.VMEM((pack, width), F32),
         pltpu.VMEM((QUARTERS * pack, lanes), BF16),
         pltpu.VMEM((n_cuts, n_group, QUARTERS * CAP, lanes), BF16),
-        pltpu.VMEM((total, QUARTERS * CAP, lanes), BF16),
+        pltpu.VMEM((n_group * n_cuts, QUARTERS * CAP, lanes), BF16),
+        pltpu.VMEM((QUARTERS * reqs, lanes), BF16),
+        pltpu.VMEM((QUARTERS * reqs, lanes), BF16),
         dma((13,)),
         dma((3, n_group)),
         dma((n_group,)),
@@ -717,8 +744,10 @@
         dma((n_group, 2)),
         dma((n_group,)),
         dma((n_group,)),
-        dma((total,)),
-        dma((total,)),
+        dma((n_group * n_cuts,)),
+        dma((n_group * n_cuts,)),
+        dma((1,)),
+        dma((1,)),
     ]
     return pl.pallas_call(
         functools.partial(layer_kernel, sizes),

time: 64.3 us -> 46.1 us (0.72)
  local copies, waits for them, and re-layouts: 10.4 us -> 1.35 us
  Pallas kernels: 52.8 us -> 44.3 us
    pallas_call x1, Pallas kernels: 52.8 us -> 44.3 us  [fused(): pl.pallas_call(functools.partial(layer_kernel, sizes), out_shape=jax.Shap...]
    unnamed x5 -> x1, local copies, waits for them, and re-layouts: 9.11 us -> 1.35 us
    reshape x1 -> x0, local copies, waits for them, and re-layouts: 1.31 us -> none  [fused(): gain = norm_gain.reshape(1, width)]
where the time goes in v2:
time: 46.1 us; the launch traced here: 45.7 us
  Pallas kernels  44.3 us (96%)
  local copies, waits for them, and re-layouts  1.35 us (3%)
    pallas_call x1, Pallas kernels, fused(): pl.pallas_call(functools.partial(layer_kernel, sizes), out_shape=jax.Shap...  44.3 us
    unnamed x1, local copies, waits for them, and re-layouts  1.35 us

profile of v2, /device:TPU:0, one launch (start us, length us, event | category | flops | bytes accessed | tf_op | source)
XLA Modules:
  0.0 45.7 jit_solution(14815087238084536777)
XLA Ops:
  0.0 44.3 %shard_map.172 = bf16[16,720]{1,0:T(8,128)(2,1)} custom-call(s32[16]{0:T(128)} %len_ref.1, f32[8]{0:T(128)} %sink_ref.1, bf16[16,512]{1,0:T(8,128)(2,1)} %q_hbm.1, bf16[16,64]{1,0:T(8,128)(2,1)} %nk_hbm.1, bf16[16,64]{1,0:T(8,128)(2,1)} %nv_hbm.1, bf16[16,64,512]{2,1,0:T(8,128)(2,1)} %bitcast.6, bf16[16,64,512]{2,1,0:T(8,128)(2,1)} %bitcast.7, ...), custom_call_target="tpu_custom_call" | custom-call | flops 796262400 | bytes 49766400 | tf_op jit(solution)/shard_map/pallas_call | solution.py:752
  44.3 1.3 %copy.20 = bf16[16,720]{1,0:T(8,128)(2,1)} copy(bf16[16,720]{1,0:T(8,128)(2,1)} %shard_map.172) | data formatting | bytes 46080

commit v3 on v2

--- a/solution.py
+++ b/solution.py
@@ -159,6 +159,7 @@
     sd,
     xd,
     xp,
+    pre,
     act,
     yb,
     yq,
@@ -223,9 +224,11 @@
             ]
         )
 
-    def fetch(m):
-        for copy in weights[m]:
-            copy.start()
+    def fetch(m, blocks):
+        for i in blocks:
+            weights[m][i].start()
+
+    early, late = range(n_group // 2), range(n_group // 2, n_group)
 
     barrier = pltpu.get_barrier_semaphore()
 
@@ -253,7 +256,7 @@
     n_rows = reqs * heads
     for copy in small[:4]:
         copy.wait()
-    fetch(0)
+    fetch(0, range(n_group))
     q = q_v[...]
     q_stack = jnp.concatenate([q[:, h * hd : (h + 1) * hd] for h in range(heads)], axis=0)
     q_rows = dot(swap_digits(heads, reqs, 1, BF16), q_stack)
@@ -312,6 +315,8 @@
         copy.start()
         sends.append(copy)
 
+    fetch(1, early)
+
     for copy in small[5:]:
         copy.wait()
     eye = hot(iota((reqs, reqs), 0) == iota((reqs, reqs), 1)).astype(BF16)
@@ -339,10 +344,6 @@
     )
     place_rows = jnp.where(same_blk, place_rows, 0.0).astype(BF16)
     resid = resid_v[...]
-    router_t, ain_t = router_v[...], ain_v[...]
-    for i in range(n_group):
-        rs[i, :experts] = router_t[:, i * blk : (i + 1) * blk]
-        rs[i, experts:] = ain_t[:, i * blk : (i + 1) * blk]
 
     for i in range(1, n_group):
         peer = lax.rem(g + i, n_group)
@@ -372,7 +373,7 @@
         )
         copy.start()
         sends.append(copy)
-    fetch(1)
+    fetch(1, late)
     row_block, col_half = lax.div(d, 2), lax.rem(d, 2)
     total_block = pb[
         pl.ds(pl.multiple_of(row_block * reqs, reqs), reqs),
@@ -414,7 +415,11 @@
         else:
             send_sum()
 
-    fetch(2)
+    fetch(2, early)
+    router_t, ain_t = router_v[...], ain_v[...]
+    for i in range(n_group):
+        rs[i, :experts] = router_t[:, i * blk : (i + 1) * blk]
+        rs[i, experts:] = ain_t[:, i * blk : (i + 1) * blk]
 
     def sums_from(i, h):
         pos = 2 * g + h
@@ -465,6 +470,7 @@
         )
         copy.start()
         sends.append(copy)
+    fetch(2, late)
     xd[g] = sd[g]
 
     logits = jnp.zeros((reqs, experts), F32)
@@ -522,9 +528,8 @@
             x = xp[i * pack : (i + 1) * pack, :blk]
             pre_gate = pre_gate + dot(x, wg_v[i * blk : (i + 1) * blk, cols])
             pre_up = pre_up + dot(x, wu_v[i * blk : (i + 1) * blk, cols])
-        act[:, cols] = (
-            (pre_up + 1.0) * pre_gate * jax.nn.sigmoid(1.702 * pre_gate)
-        ).astype(BF16)
+        pre[0, :, cols] = pre_gate
+        pre[1, :, cols] = pre_up
 
     step = 512
     full = ff // step
@@ -536,25 +541,29 @@
     lax.fori_loop(0, full, hidden_step, 0)
     if ff % step:
         hidden_cols(pl.ds(full * step, ff - full * step))
+    pre_gate, pre_up = pre[0], pre[1]
+    act[...] = ((pre_up + 1.0) * pre_gate * jax.nn.sigmoid(1.702 * pre_gate)).astype(BF16)
 
     for copy in weights[2]:
         copy.wait()
     chunk = 2 * half
-    for k in range(n_cuts):
+
+    def down(k):
         low_col, high_col = k * chunk, min((k + 1) * chunk, width)
         yb[:, low_col:high_col] = dot(act[...], wd_v[:, low_col:high_col])
-        values = yb[...]
+
+    down(0)
+    for k in range(n_cuts):
+        begin = k * blk // 128 * 128
+        values = yb[:, begin : min((k + 1) * chunk, width)]
         for i in range(QUARTERS):
-            begin = k * blk + i * part
-            yq[i * pack : (i + 1) * pack, :part] = values[:, begin : begin + part].astype(BF16)
+            at_col = k * blk + i * part - begin
+            yq[i * pack : (i + 1) * pack, :part] = values[:, at_col : at_col + part].astype(BF16)
+        if k < n_cuts - 1:
+            down(k + 1)
         blocks = dot(swap, yq[...]).astype(BF16)
         for i in range(n_group):
             se[k, i] = blocks[i * pack : (i + 1) * pack]
-
-        @pl.when(c == k)
-        def _(k=k):
-            re[mine_e] = se[k, g]
-
         for dg in range(n_group):
             to_g = lax.rem(g + dg, n_group)
 
@@ -572,6 +581,7 @@
                 pl.when(c != k)(send_rows)
             else:
                 send_rows()
+    re[mine_e] = se[c, g]
 
     def other_of(i):
         peer = lax.rem(mine_e + i, flank)
@@ -727,6 +737,7 @@
         pltpu.VMEM((n_group, pack, 2 * half), BF16),
         pltpu.VMEM((n_group, pack, 2 * half), BF16),
         pltpu.VMEM((n_group * pack, 2 * half), BF16),
+        pltpu.VMEM((2, pack, ff), F32),
         pltpu.VMEM((pack, ff), BF16),
         pltpu.VMEM((pack, width), F32),
         pltpu.VMEM((QUARTERS * pack, lanes), BF16),

time: 46.1 us -> 46.2 us (level)
  no operation moved by 1% of the time
where the time goes in v3:
time: 46.2 us; the launch traced here: 46 us
  Pallas kernels  44.6 us (97%)
  local copies, waits for them, and re-layouts  1.35 us (3%)
    pallas_call x1, Pallas kernels, fused(): pl.pallas_call(functools.partial(layer_kernel, sizes), out_shape=jax.Shap...  44.6 us
    unnamed x1, local copies, waits for them, and re-layouts  1.35 us

profile of v3, /device:TPU:0, one launch (start us, length us, event | category | flops | bytes accessed | tf_op | source)
XLA Modules:
  0.0 46.0 jit_solution(1913561992045156666)
XLA Ops:
  0.0 44.6 %shard_map.172 = bf16[16,720]{1,0:T(8,128)(2,1)} custom-call(s32[16]{0:T(128)} %len_ref.1, f32[8]{0:T(128)} %sink_ref.1, bf16[16,512]{1,0:T(8,128)(2,1)} %q_hbm.1, bf16[16,64]{1,0:T(8,128)(2,1)} %nk_hbm.1, bf16[16,64]{1,0:T(8,128)(2,1)} %nv_hbm.1, bf16[16,64,512]{2,1,0:T(8,128)(2,1)} %bitcast.6, bf16[16,64,512]{2,1,0:T(8,128)(2,1)} %bitcast.7, ...), custom_call_target="tpu_custom_call" | custom-call | flops 796262400 | bytes 49766400 | tf_op jit(solution)/shard_map/pallas_call | solution.py:763
  44.6 1.3 %copy.20 = bf16[16,720]{1,0:T(8,128)(2,1)} copy(bf16[16,720]{1,0:T(8,128)(2,1)} %shard_map.172) | data formatting | bytes 46080
